TPU v7x, 256 devices: a whole 4x4x8 slice. The times are simulated.
256 devices in a mesh: dp: 64 (over x, z, core), mp: 4 (over y).
Axes of the slice: x: 4, y: 4, z: 8, core: 2. Of those that a mesh axis runs over, the one named last changes fastest.
Arguments:
- activations: bfloat16 [32768, 2560], P('dp'), may hold values from -6 to 6
- cotangent: bfloat16 [32768, 6912], P('dp', 'mp'), may hold values from -6 to 6
- frozen_weight: bfloat16 [2560, 6912], P(None, 'mp'), may hold values from -0.078125 to 0.078125
- skew_params: bfloat16 [10, 256, 256], replicated, may hold values from -0.125 to 0.125
- tile_order: int32 [20], replicated, may hold values from 0 to 19, each once
- block_owner: int32 [10], replicated, may hold values from 0 to 63, as said below
Outputs:
- input_grad: bfloat16 [32768, 2560], P('dp', 'mp')
- skew_grads: float32 [192, 256, 256], P('dp')
Inputs may be any that keep to these rules, and one draw needn't show every extreme that they name: `tile_order`: a permutation of the 20 tiles. `block_owner`: no index of dp owns more than 3 blocks, and some index owns exactly 3; indices 0 and 64 - 1 own blocks in every draw.
All inputs are finite; a program needn't handle non-finite values.
Results may differ from a plain program's by a relative error of at most 0.001.
Values sent between devices are 32-bit elements; how exact they have to be, the bound alone decides.
No kernel may reach another device: no remote copies, remote signals or barrier semaphores. Data moves between devices by JAX's collectives and lax.ppermute only.
A program may use at most 128 MiB of HBM per device.

v0:
```python
import math
import jax
import jax.numpy as jnp
from jax import lax
from jax.sharding import PartitionSpec as P

SLOTS = 3
highest = lax.Precision.HIGHEST


def product(first, second):
    return jnp.einsum("bij,bjk->bik", first, second, precision=highest)


def cayley_parts(params):
    plain = params.astype(jnp.float32)
    skew = plain - jnp.swapaxes(plain, 1, 2)
    square = product(skew, skew)
    cube = product(square, skew)
    identity = jnp.eye(skew.shape[1], dtype=jnp.float32)
    return (skew, identity[None] + 2.0 * skew + 2.0 * square + cube)


def to_blocks(matrix, order, tile_count, block_count):
    tiled = matrix.reshape(matrix.shape[0], tile_count, -1)
    return jnp.take(tiled, order, axis=1).reshape(matrix.shape[0], block_count, -1)


def inverse_order(order, tile_count):
    positions = jnp.arange(tile_count, dtype=jnp.int32)
    matches = (order[:, None] == positions[None, :]).astype(jnp.int32)
    return jnp.sum(positions[:, None] * matches, axis=0)


def adjoint(gram, skew):
    transposed = jnp.swapaxes(skew, 1, 2)
    left = product(gram, transposed)
    right = product(transposed, gram)
    total = (
        2.0 * gram
        + 2.0 * (left + right)
        + product(left, transposed)
        + product(transposed, left)
        + product(transposed, right)
    )
    return total - jnp.swapaxes(total, 1, 2)


def local(activations, cotangent, frozen_weight, skew_params, tile_order, block_owner):
    token_rows = activations.shape[0]
    tile_count = tile_order.shape[0]
    block_count = block_owner.shape[0]
    skew, rotation = cayley_parts(skew_params)
    partial_grad = lax.dot_general(
        cotangent, frozen_weight, (((1,), (1,)), ((), ())), preferred_element_type=jnp.float32
    )
    feature_grad = lax.psum(partial_grad, "mp")
    grad_blocks = to_blocks(feature_grad, tile_order, tile_count, block_count)
    own_tiles = tile_count // lax.axis_size("mp")
    inverse = inverse_order(tile_order, tile_count)
    own_places = lax.dynamic_slice_in_dim(inverse, lax.axis_index("mp") * own_tiles, own_tiles, 0)
    half_rows = rotation.reshape(block_count * 2, rotation.shape[1] // 2, rotation.shape[2])
    own_rotation = jnp.take(half_rows, own_places, axis=0)
    own_blocks = jnp.take(grad_blocks, own_places // 2, axis=1)
    own_rotated = jnp.einsum("tkj,kij->tki", own_blocks, own_rotation, precision=highest)
    input_grad = own_rotated.reshape(token_rows, -1).astype(jnp.bfloat16)
    quarter = token_rows // lax.axis_size("mp")
    row_start = lax.axis_index("mp") * quarter
    some_inputs = lax.dynamic_slice_in_dim(activations, row_start, quarter, 0)
    input_blocks = to_blocks(some_inputs, tile_order, tile_count, block_count).astype(jnp.float32)
    some_grads = lax.dynamic_slice_in_dim(grad_blocks, row_start, quarter, 0)
    local_gram = jnp.einsum("tbi,tbj->bij", input_blocks, some_grads, precision=highest)
    gram = lax.psum(local_gram, ("dp", "mp"))
    owned = (block_owner == lax.axis_index("dp")).astype(jnp.int32)
    ranking = jnp.cumsum(owned) - 1
    slot_ids = jnp.arange(SLOTS, dtype=jnp.int32)
    selector = ((owned[None, :] == 1) & (ranking[None, :] == slot_ids[:, None])).astype(jnp.float32)
    gram_slots = jnp.einsum("sb,bij->sij", selector, gram, precision=highest)
    skew_slots = jnp.einsum("sb,bij->sij", selector, skew, precision=highest)
    scaling = 1.0 / math.sqrt(token_rows * lax.axis_size("dp"))
    skew_grads = adjoint(gram_slots, skew_slots) * scaling
    return (input_grad, skew_grads)


def solution(mesh):
    placed = (P("dp", None), P("dp", "mp"), P(None, "mp"), P(), P(), P())
    return jax.shard_map(
        local,
        mesh=mesh,
        in_specs=placed,
        out_specs=(P("dp", "mp"), P("dp", None, None)),
        check_vma=False,
    )
```

profile of v0, /device:TPU:2, one launch (start us, length us, event | category | flops | bytes accessed | tf_op | source)
XLA Modules:
  0.0 453.6 jit_solution(274264501818761207)
XLA Ops:
  7.2 0.0 copy-start
  7.2 0.0 all-reduce.3.cloned.1.call-start
  7.2 11.4 %fusion.34 = f32[512,2560]{0,1:T(8,128)} fusion(bf16[512,1728]{0,1:T(8,128)(2,1)} %param.7, bf16[2560,1728]{0,1:T(8,128)(2,1)} %param.8), kind=kOutput, calls=%fused_computation.62 | convolution fusion | flops 4529848320 | bytes 15859712 | tf_op jit(solution)/shard_map/dot_general | solution.py:54
  18.7 5.9 %copy.80 = f32[512,20,128]{2,0,1:T(8,128)} copy(f32[512,20,128]{0,2,1:T(8,128)} %bitcast.49) | data formatting | bytes 10485760 | tf_op jit(solution)/shard_map/reshape | solution.py:25
  24.6 0.0 copy-start.5
  24.6 0.0 copy-start.6
  24.6 0.0 all-reduce.3.cloned.1.call-update
  24.6 0.0 all-reduce.5.cloned.1.call-start
  24.7 0.6 copy-done.5
  25.3 0.2 reduce-window.8
  25.4 0.0 copy-done.6
  25.5 0.1 broadcast_in_dim.63
  25.5 0.1 broadcast_in_dim.64
  25.7 0.0 copy-done
  25.7 0.1 constant_dynamic-slice_fusion
  25.7 0.3 copy.100
  26.1 0.3 copy.84
  26.4 0.7 gather_fusion.3
  27.1 0.3 copy.85
  27.4 1.6 copy.77
  29.0 0.0 copy-start.4
  29.1 1.9 copy.78
  31.0 0.1 select_reduce_fusion
  31.1 0.1 compare_and_fusion.2
  31.2 0.0 copy-done.4
  31.2 0.5 bitcast_select_fusion
  31.7 2.4 bitcast_subtract_fusion
  34.1 3.9 fusion
  38.0 104.7 %all-reduce.3.cloned.1.call-done = f32[512,20,128]{2,0,1:T(8,128)} async-done(((f32[512,20,128]{2,0,1:T(8,128)}), f32[512,20,128]{2,0,1:T(8,128)}) %all-reduce.3.cloned.1.call-update) | async-done | bytes 5242896 | tf_op jit(solution)/shard_map/psum | solution.py:57
  142.7 5.7 %gather_fusion.1 = f32[20,512,128]{2,1,0:T(8,128)} fusion(f32[512,20,128]{2,0,1:T(8,128)} %all-reduce.3.cloned.1.call-done, s32[1024]{0:T(1024)S(1)} %pad_clamp_fusion.1), kind=kCustom, calls=%fused_computation.1 | custom fusion | bytes 10485840 | tf_op jit(solution)/shard_map/jit(_take)/gather | solution.py:26
  148.4 5.9 %copy.81 = f32[512,20,128]{0,2,1:T(8,128)} copy(f32[512,20,128]{2,0,1:T(8,128)} %bitcast.47) | data formatting | bytes 10485760 | tf_op jit(solution)/shard_map/jit(_take)/gather | solution.py:26
  154.3 5.9 %copy.82 = f32[512,10,256]{2,0,1:T(8,128)} copy(f32[512,10,256]{0,2,1:T(8,128)} %bitcast.48) | data formatting | bytes 10485760 | tf_op jit(solution)/shard_map/jit(_take)/gather | solution.py:26
  160.2 2.9 broadcast_select_fusion
  163.1 0.0 copy-start.2
  163.1 2.3 copy-done.2
  165.4 2.8 fusion.11
  168.2 0.0 all-reduce.5.cloned.1.call-update
  168.3 1.5 copy.90
  169.8 2.9 fusion.33
  172.7 4.8 %add_add_fusion = f32[10,256,256]{2,1,0:T(8,128)} fusion(f32[10,256,256]{2,1,0:T(8,128)S(1)} %fusion.33, f32[10,256,256]{2,1,0:T(8,128)S(1)} %bitcast_subtract_fusion, f32[256,256]{1,0:T(8,128)S(1)} %fusion.24), kind=kOutput, calls=%fused_computation.13 | convolution fusion | flops 2016542720 | bytes 8126464 | tf_op jit(solution)/shard_map/bij,bjk->bik/dot_general | solution.py:12
  177.4 3.2 gather_fusion
  180.6 3.2 gather_fusion.2
  183.8 4.7 %fusion.7 = bf16[5,128,512]{2,1,0:T(8,128)(2,1)} fusion(f32[5,512,256]{2,1,0:T(8,128)S(1)} %gather_fusion.2, pred[5]{0:T(512)(128)(4,1)S(1)} %get-tuple-element.16, f32[5,128,256]{2,1,0:T(8,128)} %gather_fusion, pred[5]{0:T(512)(128)(4,1)S(1)} %get-tuple-element.10), kind=kOutput, calls=%fused_computation.14 | convolution fusion | flops 1007779840 | bytes 3932170 | tf_op jit(solution)/shard_map/tkj,kij->tki/dot_general | solution.py:65
  188.5 2.2 copy.97
  190.7 0.0 copy-start.3
  190.7 240.4 %all-reduce.5.cloned.1.call-done = f32[10,256,256]{2,1,0:T(8,128)} async-done(((f32[10,256,256]{2,1,0:T(8,128)}), f32[10,256,256]{2,1,0:T(8,128)}) %all-reduce.5.cloned.1.call-update) | async-done | bytes 2621456 | tf_op jit(solution)/shard_map/psum | solution.py:73
  431.1 4.8 %fusion.2 = f32[3,256,256]{2,0,1:T(4,128)S(1)} fusion(f32[10,256,256]{2,1,0:T(8,128)} %all-reduce.5.cloned.1.call-done, s32[10]{0:T(128)S(1)} %add_bitcast_fusion, pred[10]{0:T(512)(128)(4,1)S(1)} %get-tuple-element.14), kind=kOutput, calls=%fused_computation.6 | convolution fusion | flops 23593020 | bytes 3407922 | tf_op jit(solution)/shard_map/sb,bij->sij/dot_general | solution.py:78
  436.0 0.0 copy-done.3
  436.0 1.0 fusion.17
  437.0 1.0 fusion.19
  438.0 1.1 convolution_add_fusion.2
  439.1 0.9 convolution_add_fusion.1
  440.1 0.0 copy-start.1
  440.1 1.8 convolution_add_fusion
  441.9 2.3 copy.96
  444.2 1.5 fusion.14
  445.6 1.1 copy.98
  446.8 0.0 copy-done.1
  (9 shorter events, 0.1 us)
Async XLA Ops:
  7.2 18.5 %copy-start = (bf16[512,2560]{1,0:T(8,128)(2,1)S(1)}, bf16[512,2560]{1,0:T(8,128)(2,1)}, u32[]{:S(2)}) copy-start(bf16[512,2560]{1,0:T(8,128)(2,1)} %param.6) | copy-start | bytes 7864324
  7.2 135.6 %all-reduce.3.cloned.1.call-start = ((), (), s32[]{:S(2)}) async-start(), calls=%async_computation | async-start | bytes 10485760 | tf_op jit(solution)/shard_map/psum | solution.py:57
  24.6 0.7 copy-start.5
  24.6 0.8 copy-start.6
  24.6 406.5 %all-reduce.5.cloned.1.call-start = ((), (), s32[]{:S(2)}) async-start(), calls=%async_computation.1 | async-start | bytes 5242880 | tf_op jit(solution)/shard_map/psum | solution.py:73
  29.0 2.1 copy-start.4
  163.1 2.3 copy-start.2
  190.7 245.2 %copy-start.3 = (f32[3,256,256]{2,0,1:T(4,128)S(1)}, f32[3,256,256]{2,0,1:T(4,128)}, u32[]{:S(2)}) copy-start(f32[3,256,256]{2,0,1:T(4,128)} %fusion) | copy-start | bytes 2359300
  440.1 6.7 %copy-start.1 = (bf16[512,2560]{1,0:T(8,128)(2,1)S(1)}, bf16[512,2560]{1,0:T(8,128)(2,1)}, u32[]{:S(2)}) copy-start(bf16[512,2560]{1,0:T(8,128)(2,1)} %param.6) | copy-start | bytes 7864324
Sparse Core Ops, SparseCore 0:
  24.7 117.9 all-reduce.2
  168.4 262.7 all-reduce.4
where the time goes:
time: 454 us
  waiting for transfers between devices  345 us (76%)
  local copies, waits for them, and re-layouts  45.2 us (10%)
  matrix products  41.2 us (9%)
  between operations  14.3 us (3%)
  other arithmetic  7.66 us (2%)
    psum x1, waiting for transfers between devices, local(): gram = lax.psum(local_gram, ('dp', 'mp'))  240 us
    psum x1, waiting for transfers between devices, local(): feature_grad = lax.psum(partial_grad, 'mp')  105 us
    gather x5, local copies, waits for them, and re-layouts, to_blocks(): jnp.take(tiled, order, axis=1).reshape(matrix.shape[0], block_count, -1)  18.5 us
    dot_general x7, matrix products, product(): return jnp.einsum('bij,bjk->bik', first, second, precision=highest)  13.5 us
    dot_general x1, matrix products, local(): lax.dot_general(cotangent, frozen_weight, (((1,), (1,)), ((), ())), prefe...  11.4 us
  transfers between devices with their start and end apart: 2, of which 2 were waited for; matrix products, arithmetic and copies ran while one was open for 8% of the time, Pallas kernels for 0%

commit v1 on v0

--- a/solution.py
+++ b/solution.py
@@ -54,7 +54,10 @@
     partial_grad = lax.dot_general(
         cotangent, frozen_weight, (((1,), (1,)), ((), ())), preferred_element_type=jnp.float32
     )
-    feature_grad = lax.psum(partial_grad, "mp")
+    size, feature_grad = (lax.axis_size("mp"), partial_grad)
+    for stride in [1 << k for k in range(size.bit_length() - 1)]:
+        swap = [(i, i ^ stride) for i in range(size)]
+        feature_grad = feature_grad + lax.ppermute(feature_grad, "mp", swap)
     grad_blocks = to_blocks(feature_grad, tile_order, tile_count, block_count)
     own_tiles = tile_count // lax.axis_size("mp")
     inverse = inverse_order(tile_order, tile_count)

time: 454 us -> 583 us (1.28)
  waiting for transfers between devices: 345 us -> 456 us
  other arithmetic: 7.66 us -> 18.3 us
    ppermute x0 -> x2, waiting for transfers between devices: none -> 213 us  [local(): feature_grad = feature_grad + lax.ppermute(feature_grad, 'mp', swap)]
    psum x1 -> x0, waiting for transfers between devices: 105 us -> none  [local(): feature_grad = lax.psum(partial_grad, 'mp')]
    add x0 -> x2, other arithmetic: none -> 10.6 us  [local(): feature_grad = feature_grad + lax.ppermute(feature_grad, 'mp', swap)]
    add x0 -> x1, local copies, waits for them, and re-layouts: none -> 5.9 us  [local(): feature_grad = feature_grad + lax.ppermute(feature_grad, 'mp', swap)]
  transfers between devices with their start and end apart: 2 -> 3, of which waited for: 2 -> 3; matrix products, arithmetic and copies ran while one was open for 8% -> 6% of each run, Pallas kernels for 0% -> 0%
where the time goes in v1:
time: 583 us
  waiting for transfers between devices  456 us (78%)
  local copies, waits for them, and re-layouts  50.7 us (9%)
  matrix products  38 us (7%)
  other arithmetic  18.3 us (3%)
  between operations  14.3 us (2%)
    psum x1, waiting for transfers between devices, local(): gram = lax.psum(local_gram, ('dp', 'mp'))  243 us
    ppermute x2, waiting for transfers between devices, local(): feature_grad = feature_grad + lax.ppermute(feature_grad, 'mp', swap)  213 us
    gather x5, local copies, waits for them, and re-layouts, to_blocks(): jnp.take(tiled, order, axis=1).reshape(matrix.shape[0], block_count, -1)  18.5 us
    dot_general x7, matrix products, product(): return jnp.einsum('bij,bjk->bik', first, second, precision=highest)  13.5 us
  transfers between devices with their start and end apart: 3, of which 3 were waited for; matrix products, arithmetic and copies ran while one was open for 6% of the time, Pallas kernels for 0%

profile of v1, /device:TPU:2, one launch (start us, length us, event | category | flops | bytes accessed | tf_op | source)
XLA Modules:
  0.0 582.6 jit_solution(14605904334856753786)
XLA Ops:
  7.2 0.0 copy-start
  7.2 0.0 all-reduce.2.cloned.1.call-start
  7.2 8.3 %fusion.34 = f32[512,2560]{1,0:T(8,128)S(1)} fusion(bf16[512,1728]{0,1:T(8,128)(2,1)} %param.7, bf16[2560,1728]{0,1:T(8,128)(2,1)} %param.8), kind=kOutput, calls=%fused_computation.62 | convolution fusion | flops 4529848320 | bytes 15859712 | tf_op jit(solution)/shard_map/dot_general | solution.py:54
  15.5 1.7 collective-permute-start
  17.2 113.2 %collective-permute-done = f32[512,2560]{1,0:T(8,128)S(1)} collective-permute-done((f32[512,2560]{1,0:T(8,128)S(1)}, f32[512,2560]{1,0:T(8,128)S(1)}, u32[]{:S(2)}, u32[]{:S(2)}) %collective-permute-start) | collective-permute-done | bytes 5242912 | tf_op jit(solution)/shard_map/ppermute | solution.py:60
  130.4 3.3 add.88
  133.7 0.0 copy-start.6
  133.7 3.2 collective-permute-start.1
  136.9 0.0 copy-done
  136.9 0.0 copy-start.5
  136.9 0.3 copy.99
  137.2 0.3 copy.84
  137.6 0.0 copy-done.6
  137.6 0.7 gather_fusion.3
  138.3 0.3 copy.85
  138.7 0.1 broadcast_in_dim.63
  138.7 0.1 broadcast_in_dim.64
  138.9 0.0 copy-done.5
  138.9 0.2 reduce-window.8
  139.1 1.6 copy.77
  140.7 0.0 copy-start.4
  140.7 1.9 copy.78
  142.6 0.1 select_reduce_fusion
  142.7 0.1 compare_and_fusion.2
  142.8 0.0 copy-done.4
  142.8 0.5 bitcast_select_fusion
  143.3 2.4 bitcast_subtract_fusion
  145.7 3.9 fusion
  149.6 99.8 %collective-permute-done.1 = f32[512,2560]{1,0:T(8,128)} collective-permute-done((f32[512,2560]{1,0:T(8,128)}, f32[512,2560]{1,0:T(8,128)}, u32[]{:S(2)}, u32[]{:S(2)}) %collective-permute-start.1) | collective-permute-done | bytes 5242912 | tf_op jit(solution)/shard_map/ppermute | solution.py:60
  249.4 7.3 %add.89 = f32[512,2560]{1,0:T(8,128)} add(f32[512,2560]{1,0:T(8,128)} %add.88, f32[512,2560]{1,0:T(8,128)} %collective-permute-done.1) | non-fusion elementwise | flops 1310720 | bytes 15728640 | tf_op jit(solution)/shard_map/add | solution.py:60
  256.7 5.9 %copy.79 = f32[512,2560]{0,1:T(8,128)} copy(f32[512,2560]{1,0:T(8,128)} %add.89) | data formatting | bytes 10485760 | tf_op jit(solution)/shard_map/add | solution.py:60
  262.6 5.9 %copy.80 = f32[512,20,128]{2,0,1:T(8,128)} copy(f32[512,20,128]{0,2,1:T(8,128)} %bitcast.48) | data formatting | bytes 10485760 | tf_op jit(solution)/shard_map/reshape | solution.py:25
  268.6 5.7 gather_fusion.1
  274.2 5.9 %copy.81 = f32[512,20,128]{0,2,1:T(8,128)} copy(f32[512,20,128]{2,0,1:T(8,128)} %bitcast.47) | data formatting | bytes 10485760 | tf_op jit(solution)/shard_map/jit(_take)/gather | solution.py:26
  280.2 5.9 %copy.82 = f32[512,10,256]{2,0,1:T(8,128)} copy(f32[512,10,256]{0,2,1:T(8,128)} %bitcast.49) | data formatting | bytes 10485760 | tf_op jit(solution)/shard_map/jit(_take)/gather | solution.py:26
  286.1 2.9 broadcast_select_fusion
  289.0 0.0 copy-start.2
  289.0 2.3 copy-done.2
  291.3 2.8 fusion.11
  294.1 0.0 all-reduce.2.cloned.1.call-update
  294.1 1.5 copy.90
  295.6 2.9 fusion.33
  298.5 4.8 add_add_fusion
  303.3 3.2 gather_fusion
  306.4 3.4 gather_fusion.2
  309.8 4.7 fusion.7
  314.5 2.2 copy.97
  316.7 0.0 copy-start.3
  316.7 243.3 %all-reduce.2.cloned.1.call-done = f32[10,256,256]{2,1,0:T(8,128)} async-done(((f32[10,256,256]{2,1,0:T(8,128)}), f32[10,256,256]{2,1,0:T(8,128)}) %all-reduce.2.cloned.1.call-update) | async-done | bytes 2621456 | tf_op jit(solution)/shard_map/psum | solution.py:76
  560.1 4.9 fusion.2
  564.9 0.0 copy-done.3
  564.9 1.0 fusion.17
  566.0 1.0 fusion.19
  567.0 1.1 convolution_add_fusion.2
  568.1 0.9 convolution_add_fusion.1
  569.0 0.0 copy-start.1
  569.0 1.8 convolution_add_fusion
  570.8 2.3 copy.96
  573.1 1.5 fusion.14
  574.6 1.1 copy.98
  575.7 0.0 copy-done.1
  (10 shorter events, 0.1 us)
Async XLA Ops:
  7.2 129.7 %copy-start = (bf16[512,2560]{1,0:T(8,128)(2,1)S(1)}, bf16[512,2560]{1,0:T(8,128)(2,1)}, u32[]{:S(2)}) copy-start(bf16[512,2560]{1,0:T(8,128)(2,1)} %param.6) | copy-start | bytes 7864324
  7.2 552.9 %all-reduce.2.cloned.1.call-start = ((), (), s32[]{:S(2)}) async-start(), calls=%async_computation | async-start | bytes 5242880 | tf_op jit(solution)/shard_map/psum | solution.py:76
  15.5 114.9 %collective-permute-start = (f32[512,2560]{1,0:T(8,128)S(1)}, f32[512,2560]{1,0:T(8,128)S(1)}, u32[]{:S(2)}, u32[]{:S(2)}) collective-permute-start(f32[512,2560]{1,0:T(8,128)S(1)} %fusion.34), channel_id=1, source_target_pairs={{0,1},{1,0},{2,3},{3,2},{4,5},{5,4},{6,7},{7,6},{8,9},{9,8},{10,11... | collective-permute-start | bytes 15728648 | tf_op jit(solution)/shard_map/ppermute | solution.py:60
  133.7 3.9 copy-start.6
  133.7 115.7 %collective-permute-start.1 = (f32[512,2560]{1,0:T(8,128)}, f32[512,2560]{1,0:T(8,128)}, u32[]{:S(2)}, u32[]{:S(2)}) collective-permute-start(f32[512,2560]{1,0:T(8,128)} %add.88), channel_id=1, source_target_pairs={{0,2},{1,3},{2,0},{3,1},{4,6},{5,7},{6,4},{7,5},{8,10},{9,11},{10,... | collective-permute-start | bytes 15728648 | tf_op jit(solution)/shard_map/ppermute | solution.py:60
  136.9 2.0 copy-start.5
  140.7 2.1 copy-start.4
  289.0 2.3 copy-start.2
  316.7 248.2 %copy-start.3 = (f32[3,256,256]{2,0,1:T(4,128)S(1)}, f32[3,256,256]{2,0,1:T(4,128)}, u32[]{:S(2)}) copy-start(f32[3,256,256]{2,0,1:T(4,128)} %fusion) | copy-start | bytes 2359300
  569.0 6.7 %copy-start.1 = (bf16[512,2560]{1,0:T(8,128)(2,1)S(1)}, bf16[512,2560]{1,0:T(8,128)(2,1)}, u32[]{:S(2)}) copy-start(bf16[512,2560]{1,0:T(8,128)(2,1)} %param.6) | copy-start | bytes 7864324
Sparse Core Ops, SparseCore 0:
  294.2 265.8 all-reduce.1
